TPU v7x, 128 devices: a whole 4x4x4 slice. The times are simulated.
128 devices in a mesh: grid: 8 (over x, core), dom: 16 (over z, y).
Axes of the slice: x: 4, y: 4, z: 4, core: 2. Of those that a mesh axis runs over, the one named last changes fastest.
Arguments:
- grid_features: bfloat16 [8, 16, 512, 474], P('grid', 'dom'), may hold values from -6 to 6
- mesh_latent: bfloat16 [8, 16, 256, 512], P('grid', 'dom'), may hold values from -6 to 6
- encode_edges: bfloat16 [8, 16, 1024, 512], P('grid', 'dom'), may hold values from -6 to 6
- encode_senders: int32 [8, 16, 1024], P('grid', 'dom'), may hold values from 448 to 4159, as said below
- encode_targets: int32 [8, 16, 1024], P('grid', 'dom'), may hold values from 0 to 256, as said below
- mesh_edges: bfloat16 [8, 16, 2048, 512], P('grid', 'dom'), may hold values from -6 to 6
- mesh_senders: int32 [8, 16, 2048], P('grid', 'dom'), may hold values from 224 to 4351, as said below
- mesh_targets: int32 [8, 16, 2048], P('grid', 'dom'), may hold values from 0 to 255
- decode_edges: bfloat16 [8, 16, 1536, 512], P('grid', 'dom'), may hold values from -6 to 6
- decode_senders: int32 [8, 16, 1536], P('grid', 'dom'), may hold values from 224 to 2079, as said below
- embed_first: bfloat16 [474, 512], replicated, may hold values from -0.25 to 0.25
- embed_second: bfloat16 [512, 512], replicated, may hold values from -0.25 to 0.25
- embed_gain: float32 [512], replicated, may hold values from 0.1 to 1.9
- encode_weights: bfloat16 [7, 512, 512], replicated, may hold values from -0.25 to 0.25
- encode_gains: float32 [2, 512], replicated, may hold values from 0.1 to 1.9
- mesh_weights: bfloat16 [2, 7, 512, 512], replicated, may hold values from -0.25 to 0.25
- mesh_gains: float32 [2, 2, 512], replicated, may hold values from 0.1 to 1.9
- decode_weights: bfloat16 [7, 512, 512], replicated, may hold values from -0.25 to 0.25
- decode_gains: float32 [2, 512], replicated, may hold values from 0.1 to 1.9
Outputs:
- grid_out: bfloat16 [8, 16, 512, 512], P('grid', 'dom')
- mesh_out: bfloat16 [8, 16, 256, 512], P('grid', 'dom')
Inputs may be any that keep to these rules, and one draw needn't show every extreme that they name: `encode_senders`: each value is r * 512 + q with r = 3 (i + 1) + j + 1 naming the block nbr offset (i, j), never a block outside the grid of partitions; for r = 4 q is any row, for r under 4 q is one of the last 64 rows of the block, for r over 4 one of the first 64. `encode_targets`: the value 256 marks an empty slot; the partitions of the first and last band fill all 1024 slots, the others the first half. `mesh_senders`: values under 9 * 256 name a neighbourhood row as for the encoder, with 256 rows a block and 32 in place of 64; larger values name row v - 2304 of the coarse table. `decode_senders`: each value names a neighbourhood row as for the encoder, with 256 rows a block and 32 in place of 64.
All inputs are finite; a program needn't handle non-finite values.
Results may differ from a plain program's by a relative error of at most 0.02.
Values may be sent and summed in bfloat16 or wider, within the bound.
A program may use at most 128 MiB of HBM per device.

v0:
```python
import jax
import jax.numpy as jnp
from jax import lax
from jax.experimental import pallas as pl
from jax.experimental.pallas import tpu as pltpu
from jax.sharding import PartitionSpec as P

L = 512
C_IN = 474
G = 512
M = 256
CO = 16
RIM_G = 64
RIM_M = 32
ENC = 1024
EDGES = 2048
DEC = 1536
LAYERS = 2
BLOCK = 256
DEC_BLOCK = 384
NODE_BLOCK = DEC_BLOCK // 3
EPS = 1e-05
MESH = pl.DeviceIdType.MESH
BF = jnp.bfloat16
F32 = jnp.float32
I32 = jnp.int32

ROW_MS, ROW_MT, ROW_DS, ROW_ES, ROW_ET = 0, 16, 32, 44, 52

ORDERS = ("yzx", "xyz", "zxy", "yxz")


def dot(a, b):
    return jnp.dot(a, b, preferred_element_type=F32)


def silu(x):
    half = 0.5 * x
    return (half + half * jnp.tanh(half)).astype(BF)


def normed(values, gain):
    centred = values - jnp.mean(values, axis=-1, keepdims=True)
    variance = jnp.mean(centred * centred, axis=-1, keepdims=True)
    return centred * lax.rsqrt(variance + EPS) * gain


def onehot(same):
    return jnp.where(same, 1.0, 0.0).astype(BF)


def kernel(
    feat_h, mlat_h, eedge_h, esnd_h, etgt_h, medge_h, msnd_h, mtgt_h, dedge_h, dsnd_h,
    ew1_h, ew2_h, eg_h, encw_h, encg_h, mw_h, mg_h, decw_h, decg_h,
    gout_h, mout_h,
    feat, mlat, eedge, esnd, etgt, medge, msnd, mtgt, dedge, dsnd,
    ew1, ew2, eg, encw, encg, mw, mg, decw, decg,
    page, wide, hot_e, hot_m, hot_d, sum_e, sum_m,
    glat, gown, grim, mown, mrim, coarse, recv, before, msgs, node, state, mout,
    in_sem, out_sem, rim_send, rim_recv, ag_send, ag_recv,
):
    band = lax.axis_index("grid")
    sector = lax.axis_index("dom")
    x, core = band // 2, band % 2
    z, y = sector // 4, sector % 4
    own = {"x": x, "y": y, "z": z}

    def place(coords, on_core):
        return (coords["x"] * 2 + on_core, coords["z"] * 4 + coords["y"])

    loads = {}

    def load(name, src, dst):
        copy = pltpu.make_async_copy(src, dst, in_sem.at[len(loads)])
        copy.start()
        loads[name] = copy

    def loaded(*names):
        for name in names:
            loads[name].wait()

    load("feat", feat_h, feat)
    load("ew1", ew1_h, ew1)
    load("ew2", ew2_h, ew2)
    load("eg", eg_h, eg)
    load("encw1", encw_h.at[pl.ds(0, 3)], encw.at[pl.ds(0, 3)])
    load("msnd", msnd_h, msnd)
    load("mtgt", mtgt_h, mtgt)
    load("dsnd", dsnd_h, dsnd)
    load("esnd", esnd_h, esnd)
    load("etgt", etgt_h, etgt)
    load("mlat", mlat_h, mlat)
    load("eedge", eedge_h, eedge)
    load("encw2", encw_h.at[pl.ds(3, 4)], encw.at[pl.ds(3, 4)])
    load("encg", encg_h, encg)
    load("mg", mg_h, mg)
    load("medge", medge_h, medge)
    load("mw0", mw_h.at[0], mw.at[0])
    load("decg", decg_h, decg)
    load("dedge", dedge_h, dedge)
    load("decw", decw_h, decw)
    load("mw1", mw_h.at[1], mw.at[1])

    def offset_of(r):
        return r // 3 - 1, r % 3 - 1

    def inside(i, j):
        row, column = band + i, sector + j
        return (row >= 0) & (row < 8) & (column >= 0) & (column < 16)

    def slot_of(r):
        return r if r < 4 else r - 1

    around = [r for r in range(9) if r != 4]

    barrier = pltpu.get_barrier_semaphore()
    met = jnp.int32(10)
    for r in around:
        i, j = offset_of(r)
        met = met + inside(i, j).astype(I32)

        @pl.when(inside(i, j))
        def _():
            pl.semaphore_signal(barrier, inc=1, device_id=(band + i, sector + j), device_id_type=MESH)

    for axis in "xyz":
        for k in range(1, 4):
            peer = place({**own, axis: (own[axis] + k) % 4}, core)
            pl.semaphore_signal(barrier, inc=1, device_id=peer, device_id_type=MESH)
    partner = place(own, 1 - core)
    pl.semaphore_signal(barrier, inc=1, device_id=partner, device_id_type=MESH)

    def rim_copy(rows, rim, width, turn, r_to):
        i, j = offset_of(r_to)
        slot = slot_of(8 - r_to)
        first = rows.shape[0] - width if r_to > 4 else 0
        return pltpu.make_async_remote_copy(
            src_ref=rows.at[pl.ds(first, width)],
            dst_ref=rim.at[pl.ds(slot * width, width)],
            send_sem=rim_send.at[turn, slot],
            recv_sem=rim_recv.at[turn, slot],
            device_id=(band + i, sector + j),
            device_id_type=MESH,
        )

    def rim_start(rows, rim, width, turn):
        for r_to in around:
            @pl.when(inside(*offset_of(r_to)))
            def _():
                rim_copy(rows, rim, width, turn, r_to).start()

            r_from = 8 - r_to
            slot = slot_of(r_from)

            @pl.when(jnp.logical_not(inside(*offset_of(r_from))))
            def _():
                rim[pl.ds(slot * width, width), :] = jnp.zeros((width, L), BF)

    def rim_wait(rows, rim, width, turn):
        for r_from in around:
            @pl.when(inside(*offset_of(r_from)))
            def _():
                rim_copy(rows, rim, width, turn, 8 - r_from).wait_recv()

    def rim_sent(rows, rim, width, turn):
        for r_to in around:
            @pl.when(inside(*offset_of(r_to)))
            def _():
                rim_copy(rows, rim, width, turn, r_to).wait_send()

    ALL = slice(None)

    def coarse_piece(turn, c, done, coords, on_core):
        at = {a: (ALL if a in done else coords[a]) for a in "xyz"}
        return coarse.at[turn, c, at["x"], on_core, at["z"], at["y"]]

    def ag_copy(turn, c, phase, k):
        order = ORDERS[c]
        sem = (c * 4 + phase) * 4 + k
        if phase < 3:
            axis = order[phase]
            piece = coarse_piece(turn, c, order[:phase], own, core)
            peer = place({**own, axis: (own[axis] + k) % 4}, core)
        else:
            axis = order[2]
            piece = coarse_piece(turn, c, order[:2], {**own, axis: (own[axis] + 4 - k) % 4}, core)
            peer = partner
        return pltpu.make_async_remote_copy(
            src_ref=piece,
            dst_ref=piece,
            send_sem=ag_send.at[turn, sem],
            recv_sem=ag_recv.at[turn, sem],
            device_id=peer,
            device_id_type=MESH,
        )

    def ag_arrived(turn, c, phase, k):
        order = ORDERS[c]
        sem = (c * 4 + phase) * 4 + k
        axis = order[min(phase, 2)]
        done = order[: min(phase, 2)]
        coords = {**own, axis: (own[axis] + 4 - k) % 4}
        piece = coarse_piece(turn, c, done, coords, core if phase < 3 else 1 - core)
        pltpu.make_async_remote_copy(
            src_ref=piece,
            dst_ref=piece,
            send_sem=ag_send.at[turn, sem],
            recv_sem=ag_recv.at[turn, sem],
            device_id=partner,
            device_id_type=MESH,
        ).wait_recv()

    def ag_step(turn, phase):
        chunks = range(4)
        if phase == 0:
            for c in chunks:
                for k in (2, 1, 3):
                    ag_copy(turn, c, 0, k).start()
        elif phase < 3:
            for c in chunks:
                for k in (1, 3, 2):
                    ag_arrived(turn, c, phase - 1, k)
                for k in (2, 1, 3):
                    ag_copy(turn, c, phase, k).start()
                if phase == 2:
                    ag_copy(turn, c, 3, 0).start()
        elif phase == 3:
            for k in (1, 3, 2):
                for c in chunks:
                    ag_arrived(turn, c, 2, k)
                    ag_copy(turn, c, 3, k).start()
        else:
            for k in (0, 1, 3, 2):
                for c in chunks:
                    ag_arrived(turn, c, 3, k)

    def ag_sent(turn):
        for c in range(4):
            for phase in range(4):
                for k in range(0 if phase == 3 else 1, 4):
                    ag_copy(turn, c, phase, k).wait_send()

    loaded("feat", "ew1")
    hidden = silu(
        lax.dot_general(feat[...], ew1[...], (((0,), (0,)), ((), ())), preferred_element_type=F32)
    )
    loaded("ew2", "eg")
    glat[...] = normed(dot(hidden, ew2[...]), eg[...]).astype(BF)
    loaded("encw1")
    gown[...] = dot(glat[...], encw[1]).astype(BF)
    pl.semaphore_wait(barrier, met)
    rim_start(gown, grim, RIM_G, 0)

    loaded("msnd", "mtgt", "dsnd", "esnd", "etgt")
    page[...] = jnp.zeros_like(page)
    for ref, row in ((msnd, ROW_MS), (mtgt, ROW_MT), (dsnd, ROW_DS), (esnd, ROW_ES), (etgt, ROW_ET)):
        for n in range(ref.shape[1] // 128):
            page[row + n : row + n + 1, :] = ref[:, n * 128 : (n + 1) * 128]
    turned = page[...].T

    def spread(row, count):
        for n in range(count):
            wide[n * 128 : (n + 1) * 128, :] = jnp.broadcast_to(
                turned[:, row + n : row + n + 1], (128, 128)
            )

    def lanes(rows):
        return lax.broadcasted_iota(I32, (rows, 128), 1)

    def hot_columns(out, first, base, count, step):
        def body(n, _):
            rows = pl.ds(pl.multiple_of(n * step, step), step)
            values = wide[rows, :]
            ids = lanes(step)
            for t, start in enumerate(base):
                column = first + t * 128
                out[rows, column : column + 128] = onehot(values == ids + start)
            return 0

        lax.fori_loop(0, count // step, body, 0)

    def near_base(total, width):
        return [4 * total + n * 128 for n in range(total // 128)]

    def hot_rim(out, first, total, width, count, step):
        def body(n, _):
            rows = pl.ds(pl.multiple_of(n * step, step), step)
            values = wide[rows, :]
            per = 128 // width
            for t in range(8 * width // 128):
                lane = lanes(step)
                slot = t * per + lane // width
                r = jnp.where(slot < 4, slot, slot + 1)
                ids = r * total + jnp.where(slot < 4, total - width, 0) + lane % width
                column = first + t * 128
                out[rows, column : column + 128] = onehot(values == ids)
            return 0

        lax.fori_loop(0, count // step, body, 0)

    def hot_targets(out, row, count):
        for n in range(count // 128):
            ids = lax.broadcasted_iota(I32, (M, 128), 0)
            out[:, n * 128 : (n + 1) * 128] = onehot(ids == page[row + n : row + n + 1, :])

    spread(ROW_ET, ENC // 128)
    hot_columns(hot_e, 0, [0, 128], ENC, 128)
    spread(ROW_ES, ENC // 128)
    hot_columns(hot_e, M, near_base(G, RIM_G), ENC, 128)
    hot_rim(hot_e, M + G, G, RIM_G, ENC, 128)
    hot_targets(sum_e, ROW_ET, ENC)
    spread(ROW_MT, EDGES // 128)
    hot_columns(hot_m, 0, [0, 128], EDGES, 128)
    spread(ROW_MS, EDGES // 128)
    hot_columns(hot_m, M, near_base(M, RIM_M), EDGES, 128)
    hot_rim(hot_m, 2 * M, M, RIM_M, EDGES, 128)
    hot_columns(hot_m, 3 * M, [9 * M + n * 128 for n in range(16)], EDGES, 128)
    hot_targets(sum_m, ROW_MT, EDGES)
    spread(ROW_DS, DEC // 128)
    hot_columns(hot_d, 0, near_base(M, RIM_M), DEC, 128)
    hot_rim(hot_d, M, M, RIM_M, DEC, 128)

    loaded("mlat", "eedge")
    recv[...] = dot(mlat[...], encw[2]).astype(BF)
    loaded("encw2", "encg")
    rim_wait(gown, grim, RIM_G, 0)

    def encode_block(n, _):
        rows = pl.ds(pl.multiple_of(n * BLOCK, BLOCK), BLOCK)
        left = jnp.concatenate([eedge[rows, :], hot_e[rows, :]], axis=1)
        right = jnp.concatenate([encw[0], recv[...], gown[...], grim[...]], axis=0)
        hidden = silu(dot(left, right))
        msgs[rows, :] = normed(dot(hidden, encw[3]), encg[0:1, :]).astype(BF)
        return 0

    lax.fori_loop(0, ENC // BLOCK, encode_block, 0)

    def node_update(rows_state, own_part, summed, weight_sum, weight_out, gain):
        inner = own_part + dot(summed.astype(BF), weight_sum)
        return (rows_state.astype(F32) + normed(dot(silu(inner), weight_out), gain)).astype(BF)

    summed = dot(sum_e[...], msgs[0:ENC, :])
    state[...] = node_update(mlat[...], dot(mlat[...], encw[4]), summed, encw[5], encw[6], encg[1:2, :])

    loaded("mg", "medge")
    for layer in range(LAYERS):
        turn = layer + 1
        loaded("mw0" if layer == 0 else "mw1")
        weights = [mw.at[layer, k] for k in range(7)]
        now = state[...]
        send = dot(now, weights[1][...]).astype(BF)
        mown[layer] = send
        for c in range(4):
            coarse[layer, c, x, core, z, y] = send[0:CO, c * 128 : (c + 1) * 128]
        ag_step(layer, 0)
        rim_start(mown.at[layer], mrim.at[layer], RIM_M, turn)
        recv[...] = dot(now, weights[2][...]).astype(BF)
        node[0:M, :] = dot(now, weights[4][...])

        def first_part(n, _):
            rows = pl.ds(pl.multiple_of(n * BLOCK, BLOCK), BLOCK)
            left = jnp.concatenate([medge[rows, :], hot_m[rows, 0 : 2 * M]], axis=1)
            right = jnp.concatenate([weights[0][...], recv[...], mown[layer]], axis=0)
            before[rows, :] = dot(left, right)
            return 0

        ag_step(layer, 1)
        lax.fori_loop(0, 3, first_part, 0)
        ag_step(layer, 2)
        lax.fori_loop(3, 8, first_part, 0)
        ag_step(layer, 3)
        rim_wait(mown.at[layer], mrim.at[layer], RIM_M, turn)
        ag_step(layer, 4)

        def second_part(n, _):
            rows = pl.ds(pl.multiple_of(n * BLOCK, BLOCK), BLOCK)
            table = jnp.concatenate([coarse[layer, c].reshape(EDGES, 128) for c in range(4)], axis=1)
            right = jnp.concatenate([mrim[layer], table], axis=0)
            hidden = silu(before[rows, :] + dot(hot_m[rows, 2 * M :], right))
            message = normed(dot(hidden, weights[3][...]), mg[layer, 0:1, :])
            if layer + 1 < LAYERS:
                medge[rows, :] = (medge[rows, :].astype(F32) + message).astype(BF)
            msgs[rows, :] = message.astype(BF)
            return 0

        lax.fori_loop(0, EDGES // BLOCK, second_part, 0)
        summed = dot(sum_m[...], msgs[...])
        state[...] = node_update(now, node[0:M, :], summed, weights[5][...], weights[6][...], mg[layer, 1:2, :])

    mesh_out = pltpu.make_async_copy(state, mout_h, out_sem.at[0])
    mesh_out.start()
    loaded("decw", "decg", "dedge")
    mown[2] = dot(state[...], decw[1]).astype(BF)
    rim_start(mown.at[2], mrim.at[2], RIM_M, 3)
    node[...] = dot(glat[...], decw[4])
    rim_sent(gown, grim, RIM_G, 0)
    gown[...] = dot(glat[...], decw[2]).astype(BF)

    edge = lax.broadcasted_iota(I32, (DEC_BLOCK, NODE_BLOCK), 0) - 3 * lax.broadcasted_iota(
        I32, (DEC_BLOCK, NODE_BLOCK), 1
    )
    repeat = onehot((edge >= 0) & (edge < 3))
    edge = lax.broadcasted_iota(I32, (NODE_BLOCK, DEC_BLOCK), 1) - 3 * lax.broadcasted_iota(
        I32, (NODE_BLOCK, DEC_BLOCK), 0
    )
    gather = onehot((edge >= 0) & (edge < 3))

    def decode_first(n, _):
        rows = pl.ds(pl.multiple_of(n * DEC_BLOCK, DEC_BLOCK), DEC_BLOCK)
        nodes = pl.ds(pl.multiple_of(n * NODE_BLOCK, NODE_BLOCK), NODE_BLOCK)
        left = jnp.concatenate([dedge[rows, :], hot_d[rows, 0:M], repeat], axis=1)
        right = jnp.concatenate([decw[0], mown[2], gown[nodes, :]], axis=0)
        before[rows, :] = dot(left, right)
        return 0

    lax.fori_loop(0, DEC // DEC_BLOCK, decode_first, 0)
    rim_wait(mown.at[2], mrim.at[2], RIM_M, 3)

    def decode_second(n, _):
        rows = pl.ds(pl.multiple_of(n * DEC_BLOCK, DEC_BLOCK), DEC_BLOCK)
        nodes = pl.ds(pl.multiple_of(n * NODE_BLOCK, NODE_BLOCK), NODE_BLOCK)
        hidden = silu(before[rows, :] + dot(hot_d[rows, M:], mrim[2]))
        message = normed(dot(hidden, decw[3]), decg[0:1, :]).astype(BF)
        summed = dot(gather, message)
        mout[nodes, :] = node_update(
            glat[nodes, :], node[nodes, :], summed, decw[5], decw[6], decg[1:2, :]
        )
        return 0

    lax.fori_loop(0, DEC // DEC_BLOCK, decode_second, 0)
    grid_out = pltpu.make_async_copy(mout, gout_h, out_sem.at[1])
    grid_out.start()

    for layer in range(LAYERS):
        ag_sent(layer)
        rim_sent(mown.at[layer], mrim.at[layer], RIM_M, layer + 1)
    rim_sent(mown.at[2], mrim.at[2], RIM_M, 3)
    mesh_out.wait()
    grid_out.wait()


def per_device(
    grid_features, mesh_latent, encode_edges, encode_senders, encode_targets,
    mesh_edges, mesh_senders, mesh_targets, decode_edges, decode_senders,
    embed_first, embed_second, embed_gain, encode_weights, encode_gains,
    mesh_weights, mesh_gains, decode_weights, decode_gains,
):
    operands = (
        jnp.swapaxes(grid_features[0, 0], 0, 1), mesh_latent[0, 0], encode_edges[0, 0],
        encode_senders[0], encode_targets[0], mesh_edges[0, 0], mesh_senders[0],
        mesh_targets[0], decode_edges[0, 0], decode_senders[0], embed_first, embed_second,
        embed_gain[None], encode_weights, encode_gains, mesh_weights, mesh_gains,
        decode_weights, decode_gains,
    )
    scratch = [pltpu.VMEM(a.shape, a.dtype) for a in operands] + [
        pltpu.VMEM((128, 128), I32),
        pltpu.VMEM((EDGES, 128), I32),
        pltpu.VMEM((ENC, M + 2 * G), BF),
        pltpu.VMEM((EDGES, 3 * M + EDGES), BF),
        pltpu.VMEM((DEC, 2 * M), BF),
        pltpu.VMEM((M, ENC), BF),
        pltpu.VMEM((M, EDGES), BF),
        pltpu.VMEM((G, L), BF),
        pltpu.VMEM((G, L), BF),
        pltpu.VMEM((8 * RIM_G, L), BF),
        pltpu.VMEM((3, M, L), BF),
        pltpu.VMEM((3, 8 * RIM_M, L), BF),
        pltpu.VMEM((LAYERS, 4, 4, 2, 4, 4, CO, 128), BF),
        pltpu.VMEM((M, L), BF),
        pltpu.VMEM((EDGES, L), F32),
        pltpu.VMEM((EDGES, L), BF),
        pltpu.VMEM((G, L), F32),
        pltpu.VMEM((M, L), BF),
        pltpu.VMEM((G, L), BF),
        pltpu.SemaphoreType.DMA((24,)),
        pltpu.SemaphoreType.DMA((2,)),
        pltpu.SemaphoreType.DMA((4, 8)),
        pltpu.SemaphoreType.DMA((4, 8)),
        pltpu.SemaphoreType.DMA((LAYERS, 64)),
        pltpu.SemaphoreType.DMA((LAYERS, 64)),
    ]
    grid_out, mesh_out = pl.pallas_call(
        kernel,
        out_shape=(
            jax.ShapeDtypeStruct((G, L), BF),
            jax.ShapeDtypeStruct((M, L), BF),
        ),
        in_specs=[pl.BlockSpec(memory_space=pl.ANY)] * len(operands),
        out_specs=(pl.BlockSpec(memory_space=pl.ANY), pl.BlockSpec(memory_space=pl.ANY)),
        scratch_shapes=scratch,
        compiler_params=pltpu.CompilerParams(
            collective_id=0, has_side_effects=True, vmem_limit_bytes=62 * 1024 * 1024
        ),
        cost_estimate=pl.CostEstimate(
            flops=60_000_000_000, bytes_accessed=21_000_000, transcendentals=4_000_000
        ),
    )(*operands)
    return (grid_out[None, None], mesh_out[None, None])


def solution(mesh):
    block, row = P("grid", "dom", None, None), P("grid", "dom", None)
    return jax.shard_map(
        per_device,
        mesh=mesh,
        in_specs=(block, block, block, row, row, block, row, row, block, row) + (P(),) * 9,
        out_specs=(block, block),
        check_vma=False,
    )
```

profile of v0, /device:TPU:1, one launch (start us, length us, event | category | flops | bytes accessed | tf_op | source)
XLA Modules:
  0.0 92.2 jit_solution(3572667320778826581)
XLA Ops:
  0.6 88.0 %shard_map.194 = (bf16[512,512]{1,0:T(8,128)(2,1)}, bf16[256,512]{1,0:T(8,128)(2,1)}) custom-call(bf16[474,512]{1,0:T(8,128)(2,1)} %bitcast.20, bf16[256,512]{1,0:T(8,128)(2,1)} %bitcast.21, bf16[1024,512]{1,0:T(8,128)(2,1)} %bitcast.19, s32[1,1024]{1,0:T(1,128)} %bitcast.25, s32[1,1024]{1,0:T(1,128)} %bitcast.26, bf16[2048,512]{1,0:T(8,128)(2,1)} %bitcast.17, ...), custom_call_target="tpu_custom_call" | custom-call | flops 60000002048 | bytes 21000000 | tf_op jit(solution)/shard_map/pallas_call | solution.py:482
  88.7 1.9 %copy.23 = bf16[1,1,512,512]{3,2,1,0:T(8,128)(2,1)} copy(bf16[1,1,512,512]{3,2,1,0:T(8,128)(2,1)} %bitcast.15) | data formatting | bytes 1048576
  90.5 1.7 %copy.24 = bf16[1,1,256,512]{3,2,1,0:T(8,128)(2,1)} copy(bf16[1,1,256,512]{3,2,1,0:T(8,128)(2,1)} %bitcast.16) | data formatting | bytes 524288
where the time goes:
time: 92.4 us; the launch traced here: 92.2 us
  Pallas kernels  88 us (95%)
  local copies, waits for them, and re-layouts  3.54 us (4%)
    pallas_call x1, Pallas kernels, per_device(): pl.pallas_call(kernel, out_shape=(jax.ShapeDtypeStruct((G, L), BF), jax.S...  88 us
    unnamed x2, local copies, waits for them, and re-layouts  3.54 us

commit v1 on v0

--- a/solution.py
+++ b/solution.py
@@ -27,8 +27,6 @@
 
 ROW_MS, ROW_MT, ROW_DS, ROW_ES, ROW_ET = 0, 16, 32, 44, 52
 
-ORDERS = ("yzx", "xyz", "zxy", "yxz")
-
 
 def dot(a, b):
     return jnp.dot(a, b, preferred_element_type=F32)
@@ -63,10 +61,6 @@
     sector = lax.axis_index("dom")
     x, core = band // 2, band % 2
     z, y = sector // 4, sector % 4
-    own = {"x": x, "y": y, "z": z}
-
-    def place(coords, on_core):
-        return (coords["x"] * 2 + on_core, coords["z"] * 4 + coords["y"])
 
     loads = {}
 
@@ -113,8 +107,22 @@
 
     around = [r for r in range(9) if r != 4]
 
+    def pick(on_zero, on_one):
+        return on_zero * (1 - core) + on_one * core
+
+    g, t = pick(z, x), pick(x, z)
+
+    def back(value):
+        return lax.rem(value + 4, 4)
+
+    def at_core(gv, tv, yv):
+        return (pick(tv, gv) * 2 + core, pick(gv, tv) * 4 + yv)
+
+    plane = [(dg, dy) for dg in (2, 1, 3, 0) for dy in (2, 1, 3, 0) if dg + dy]
+    partner = (x * 2 + 1 - core, sector)
+
     barrier = pltpu.get_barrier_semaphore()
-    met = jnp.int32(10)
+    met = jnp.int32(19)
     for r in around:
         i, j = offset_of(r)
         met = met + inside(i, j).astype(I32)
@@ -123,11 +131,11 @@
         def _():
             pl.semaphore_signal(barrier, inc=1, device_id=(band + i, sector + j), device_id_type=MESH)
 
-    for axis in "xyz":
-        for k in range(1, 4):
-            peer = place({**own, axis: (own[axis] + k) % 4}, core)
-            pl.semaphore_signal(barrier, inc=1, device_id=peer, device_id_type=MESH)
-    partner = place(own, 1 - core)
+    for dg, dy in plane:
+        peer = at_core(back(g + dg), t, back(y + dy))
+        pl.semaphore_signal(barrier, inc=1, device_id=peer, device_id_type=MESH)
+    for k in range(1, 4):
+        pl.semaphore_signal(barrier, inc=1, device_id=at_core(g, back(t + k), y), device_id_type=MESH)
     pl.semaphore_signal(barrier, inc=1, device_id=partner, device_id_type=MESH)
 
     def rim_copy(rows, rim, width, turn, r_to):
@@ -168,23 +176,7 @@
             def _():
                 rim_copy(rows, rim, width, turn, r_to).wait_send()
 
-    ALL = slice(None)
-
-    def coarse_piece(turn, c, done, coords, on_core):
-        at = {a: (ALL if a in done else coords[a]) for a in "xyz"}
-        return coarse.at[turn, c, at["x"], on_core, at["z"], at["y"]]
-
-    def ag_copy(turn, c, phase, k):
-        order = ORDERS[c]
-        sem = (c * 4 + phase) * 4 + k
-        if phase < 3:
-            axis = order[phase]
-            piece = coarse_piece(turn, c, order[:phase], own, core)
-            peer = place({**own, axis: (own[axis] + k) % 4}, core)
-        else:
-            axis = order[2]
-            piece = coarse_piece(turn, c, order[:2], {**own, axis: (own[axis] + 4 - k) % 4}, core)
-            peer = partner
+    def ag_copy(turn, piece, sem, peer):
         return pltpu.make_async_remote_copy(
             src_ref=piece,
             dst_ref=piece,
@@ -194,51 +186,64 @@
             device_id_type=MESH,
         )
 
-    def ag_arrived(turn, c, phase, k):
-        order = ORDERS[c]
-        sem = (c * 4 + phase) * 4 + k
-        axis = order[min(phase, 2)]
-        done = order[: min(phase, 2)]
-        coords = {**own, axis: (own[axis] + 4 - k) % 4}
-        piece = coarse_piece(turn, c, done, coords, core if phase < 3 else 1 - core)
-        pltpu.make_async_remote_copy(
-            src_ref=piece,
-            dst_ref=piece,
-            send_sem=ag_send.at[turn, sem],
-            recv_sem=ag_recv.at[turn, sem],
-            device_id=partner,
-            device_id_type=MESH,
-        ).wait_recv()
-
-    def ag_step(turn, phase):
-        chunks = range(4)
-        if phase == 0:
-            for c in chunks:
-                for k in (2, 1, 3):
-                    ag_copy(turn, c, 0, k).start()
-        elif phase < 3:
-            for c in chunks:
-                for k in (1, 3, 2):
-                    ag_arrived(turn, c, phase - 1, k)
-                for k in (2, 1, 3):
-                    ag_copy(turn, c, phase, k).start()
-                if phase == 2:
-                    ag_copy(turn, c, 3, 0).start()
-        elif phase == 3:
+    def group(turn, gv, tv):
+        return coarse.at[turn, pick(tv, gv), core, pick(gv, tv)]
+
+    def plane_send(turn, dg, dy):
+        piece = coarse.at[turn, x, core, z, y]
+        return ag_copy(turn, piece, dg * 4 + dy, at_core(back(g + dg), t, back(y + dy)))
+
+    def plane_come(turn, dg, dy):
+        gv = back(g - dg)
+        piece = coarse.at[turn, pick(t, gv), core, pick(gv, t), back(y - dy)]
+        return ag_copy(turn, piece, dg * 4 + dy, partner)
+
+    def line_send(turn, dg, k):
+        return ag_copy(turn, group(turn, back(g - dg), t), 16 + dg * 4 + k, at_core(g, back(t + k), y))
+
+    def line_come(turn, dg, k):
+        return ag_copy(turn, group(turn, back(g - dg), back(t - k)), 16 + dg * 4 + k, partner)
+
+    def core_send(turn, dg, k):
+        return ag_copy(turn, group(turn, back(g - dg), back(t - k)), 32 + dg * 4 + k, partner)
+
+    def core_come(turn, dg, k):
+        gv, tv = back(t - dg), back(g - k)
+        piece = coarse.at[turn, pick(gv, tv), 1 - core, pick(tv, gv)]
+        return ag_copy(turn, piece, 32 + dg * 4 + k, partner)
+
+    def ag_start(turn):
+        for dg, dy in plane:
+            plane_send(turn, dg, dy).start()
+
+    def ag_second(turn):
+        for dg in (0, 1, 3, 2):
+            for dy in (0, 1, 3, 2):
+                if dg + dy:
+                    plane_come(turn, dg, dy).wait_recv()
+            for k in (2, 1, 3):
+                line_send(turn, dg, k).start()
+            core_send(turn, dg, 0).start()
+
+    def ag_third(turn):
+        for dg in (0, 1, 3, 2):
             for k in (1, 3, 2):
-                for c in chunks:
-                    ag_arrived(turn, c, 2, k)
-                    ag_copy(turn, c, 3, k).start()
-        else:
+                line_come(turn, dg, k).wait_recv()
+                core_send(turn, dg, k).start()
+
+    def ag_last(turn):
+        for dg in (0, 1, 3, 2):
             for k in (0, 1, 3, 2):
-                for c in chunks:
-                    ag_arrived(turn, c, 3, k)
+                core_come(turn, dg, k).wait_recv()
 
     def ag_sent(turn):
-        for c in range(4):
-            for phase in range(4):
-                for k in range(0 if phase == 3 else 1, 4):
-                    ag_copy(turn, c, phase, k).wait_send()
+        for dg, dy in plane:
+            plane_send(turn, dg, dy).wait_send()
+        for dg in range(4):
+            for k in range(4):
+                if k:
+                    line_send(turn, dg, k).wait_send()
+                core_send(turn, dg, k).wait_send()
 
     loaded("feat", "ew1")
     hidden = silu(
@@ -333,7 +338,7 @@
         msgs[rows, :] = normed(dot(hidden, encw[3]), encg[0:1, :]).astype(BF)
         return 0
 
-    lax.fori_loop(0, ENC // BLOCK, encode_block, 0)
+    lax.fori_loop(0, ENC // BLOCK, encode_block, 0, unroll=4)
 
     def node_update(rows_state, own_part, summed, weight_sum, weight_out, gain):
         inner = own_part + dot(summed.astype(BF), weight_sum)
@@ -350,10 +355,8 @@
         now = state[...]
         send = dot(now, weights[1][...]).astype(BF)
         mown[layer] = send
-        for c in range(4):
-            coarse[layer, c, x, core, z, y] = send[0:CO, c * 128 : (c + 1) * 128]
-        ag_step(layer, 0)
-        rim_start(mown.at[layer], mrim.at[layer], RIM_M, turn)
+        coarse[layer, x, core, z, y] = send[0:CO]
+        ag_start(layer)
         recv[...] = dot(now, weights[2][...]).astype(BF)
         node[0:M, :] = dot(now, weights[4][...])
 
@@ -364,18 +367,16 @@
             before[rows, :] = dot(left, right)
             return 0
 
-        ag_step(layer, 1)
-        lax.fori_loop(0, 3, first_part, 0)
-        ag_step(layer, 2)
-        lax.fori_loop(3, 8, first_part, 0)
-        ag_step(layer, 3)
+        lax.fori_loop(0, EDGES // BLOCK, first_part, 0, unroll=4)
+        ag_second(layer)
+        rim_start(mown.at[layer], mrim.at[layer], RIM_M, turn)
+        ag_third(layer)
         rim_wait(mown.at[layer], mrim.at[layer], RIM_M, turn)
-        ag_step(layer, 4)
+        ag_last(layer)
 
         def second_part(n, _):
             rows = pl.ds(pl.multiple_of(n * BLOCK, BLOCK), BLOCK)
-            table = jnp.concatenate([coarse[layer, c].reshape(EDGES, 128) for c in range(4)], axis=1)
-            right = jnp.concatenate([mrim[layer], table], axis=0)
+            right = jnp.concatenate([mrim[layer], coarse[layer].reshape(8 * 16 * CO, L)], axis=0)
             hidden = silu(before[rows, :] + dot(hot_m[rows, 2 * M :], right))
             message = normed(dot(hidden, weights[3][...]), mg[layer, 0:1, :])
             if layer + 1 < LAYERS:
@@ -383,7 +384,7 @@
             msgs[rows, :] = message.astype(BF)
             return 0
 
-        lax.fori_loop(0, EDGES // BLOCK, second_part, 0)
+        lax.fori_loop(0, EDGES // BLOCK, second_part, 0, unroll=4)
         summed = dot(sum_m[...], msgs[...])
         state[...] = node_update(now, node[0:M, :], summed, weights[5][...], weights[6][...], mg[layer, 1:2, :])
 
@@ -413,7 +414,7 @@
         before[rows, :] = dot(left, right)
         return 0
 
-    lax.fori_loop(0, DEC // DEC_BLOCK, decode_first, 0)
+    lax.fori_loop(0, DEC // DEC_BLOCK, decode_first, 0, unroll=4)
     rim_wait(mown.at[2], mrim.at[2], RIM_M, 3)
 
     def decode_second(n, _):
@@ -427,7 +428,7 @@
         )
         return 0
 
-    lax.fori_loop(0, DEC // DEC_BLOCK, decode_second, 0)
+    lax.fori_loop(0, DEC // DEC_BLOCK, decode_second, 0, unroll=4)
     grid_out = pltpu.make_async_copy(mout, gout_h, out_sem.at[1])
     grid_out.start()
 
@@ -437,6 +438,11 @@
     rim_sent(mown.at[2], mrim.at[2], RIM_M, 3)
     mesh_out.wait()
     grid_out.wait()
+
+
+def hand_on(grid_in, mesh_in, grid_out, mesh_out):
+    grid_out[...] = grid_in[...]
+    mesh_out[...] = mesh_in[...]
 
 
 def per_device(
@@ -465,7 +471,7 @@
         pltpu.VMEM((8 * RIM_G, L), BF),
         pltpu.VMEM((3, M, L), BF),
         pltpu.VMEM((3, 8 * RIM_M, L), BF),
-        pltpu.VMEM((LAYERS, 4, 4, 2, 4, 4, CO, 128), BF),
+        pltpu.VMEM((LAYERS, 4, 2, 4, 4, CO, L), BF),
         pltpu.VMEM((M, L), BF),
         pltpu.VMEM((EDGES, L), F32),
         pltpu.VMEM((EDGES, L), BF),
@@ -476,8 +482,8 @@
         pltpu.SemaphoreType.DMA((2,)),
         pltpu.SemaphoreType.DMA((4, 8)),
         pltpu.SemaphoreType.DMA((4, 8)),
-        pltpu.SemaphoreType.DMA((LAYERS, 64)),
-        pltpu.SemaphoreType.DMA((LAYERS, 64)),
+        pltpu.SemaphoreType.DMA((LAYERS, 48)),
+        pltpu.SemaphoreType.DMA((LAYERS, 48)),
     ]
     grid_out, mesh_out = pl.pallas_call(
         kernel,
@@ -495,6 +501,15 @@
             flops=60_000_000_000, bytes_accessed=21_000_000, transcendentals=4_000_000
         ),
     )(*operands)
+    grid_out, mesh_out = pl.pallas_call(
+        hand_on,
+        out_shape=(
+            jax.ShapeDtypeStruct((G, L), BF),
+            jax.ShapeDtypeStruct((M, L), BF),
+        ),
+        in_specs=[pl.BlockSpec(memory_space=pltpu.VMEM)] * 2,
+        out_specs=(pl.BlockSpec(memory_space=pltpu.VMEM), pl.BlockSpec(memory_space=pltpu.VMEM)),
+    )(grid_out, mesh_out)
     return (grid_out[None, None], mesh_out[None, None])
 
 

time: 92.4 us -> 81.5 us (0.88)
  Pallas kernels: 88 us -> 80.6 us
  local copies, waits for them, and re-layouts: 3.54 us -> 0 us
    pallas_call x1, Pallas kernels: 88 us -> 78.5 us  [per_device(): pl.pallas_call(kernel, out_shape=(jax.ShapeDtypeStruct((G, L), BF), jax.S...]
    unnamed x2 -> x0, local copies, waits for them, and re-layouts: 3.54 us -> none
    pallas_call x0 -> x1, Pallas kernels: none -> 2.02 us  [per_device(): pl.pallas_call(hand_on, out_shape=(jax.ShapeDtypeStruct((G, L), BF), jax....]
where the time goes in v1:
time: 81.5 us; the launch traced here: 81.2 us
  Pallas kernels  80.6 us (99%)
    pallas_call x1, Pallas kernels, per_device(): pl.pallas_call(kernel, out_shape=(jax.ShapeDtypeStruct((G, L), BF), jax.S...  78.5 us
    pallas_call x1, Pallas kernels, per_device(): pl.pallas_call(hand_on, out_shape=(jax.ShapeDtypeStruct((G, L), BF), jax....  2.02 us

profile of v1, /device:TPU:1, one launch (start us, length us, event | category | flops | bytes accessed | tf_op | source)
XLA Modules:
  0.0 81.2 jit_solution(5492130591016579444)
XLA Ops:
  0.6 78.5 %shard_map.194 = (bf16[512,512]{1,0:T(8,128)(2,1)}, bf16[256,512]{1,0:T(8,128)(2,1)}) custom-call(bf16[474,512]{1,0:T(8,128)(2,1)} %bitcast.19, bf16[256,512]{1,0:T(8,128)(2,1)} %bitcast.20, bf16[1024,512]{1,0:T(8,128)(2,1)} %bitcast.17, s32[1,1024]{1,0:T(1,128)} %bitcast.25, s32[1,1024]{1,0:T(1,128)} %bitcast.26, bf16[2048,512]{1,0:T(8,128)(2,1)} %bitcast.15, ...), custom_call_target="tpu_custom_call" | custom-call | flops 60000002048 | bytes 21000000 | tf_op jit(solution)/shard_map/pallas_call | solution.py:488
  79.2 2.0 %shard_map.195 = (bf16[512,512]{1,0:T(8,128)(2,1)}, bf16[256,512]{1,0:T(8,128)(2,1)}) custom-call(bf16[512,512]{1,0:T(8,128)(2,1)} %get-tuple-element.6.grid_in, bf16[256,512]{1,0:T(8,128)(2,1)} %get-tuple-element.7.mesh_in), custom_call_target="tpu_custom_call" | custom-call | tf_op jit(solution)/shard_map/pallas_call | solution.py:504

commit v2 on v1

--- a/solution.py
+++ b/solution.py
@@ -17,7 +17,8 @@
 DEC = 1536
 LAYERS = 2
 BLOCK = 256
-DEC_BLOCK = 384
+WIDE = 512
+DEC_BLOCK = 768
 NODE_BLOCK = DEC_BLOCK // 3
 EPS = 1e-05
 MESH = pl.DeviceIdType.MESH
@@ -325,38 +326,57 @@
     hot_columns(hot_d, 0, near_base(M, RIM_M), DEC, 128)
     hot_rim(hot_d, M, M, RIM_M, DEC, 128)
 
-    loaded("mlat", "eedge")
+    def block_rows(n):
+        return pl.ds(pl.multiple_of(n * BLOCK, BLOCK), BLOCK)
+
+    loaded("mlat", "eedge", "encw2", "encg")
     recv[...] = dot(mlat[...], encw[2]).astype(BF)
-    loaded("encw2", "encg")
+    node[0:M, :] = dot(mlat[...], encw[4])
+
+    def encode_first(n, _):
+        rows = pl.ds(pl.multiple_of(n * WIDE, WIDE), WIDE)
+        left = jnp.concatenate([eedge[rows, :], hot_e[rows, 0 : M + G]], axis=1)
+        right = jnp.concatenate([encw[0], recv[...], gown[...]], axis=0)
+        before[rows, :] = dot(left, right)
+        return 0
+
+    lax.fori_loop(0, ENC // WIDE, encode_first, 0, unroll=2)
     rim_wait(gown, grim, RIM_G, 0)
 
-    def encode_block(n, _):
-        rows = pl.ds(pl.multiple_of(n * BLOCK, BLOCK), BLOCK)
-        left = jnp.concatenate([eedge[rows, :], hot_e[rows, :]], axis=1)
-        right = jnp.concatenate([encw[0], recv[...], gown[...], grim[...]], axis=0)
-        hidden = silu(dot(left, right))
+    def encode_second(n, _):
+        rows = pl.ds(pl.multiple_of(n * WIDE, WIDE), WIDE)
+        hidden = silu(before[rows, :] + dot(hot_e[rows, M + G :], grim[...]))
         msgs[rows, :] = normed(dot(hidden, encw[3]), encg[0:1, :]).astype(BF)
         return 0
 
-    lax.fori_loop(0, ENC // BLOCK, encode_block, 0, unroll=4)
+    lax.fori_loop(0, ENC // WIDE, encode_second, 0, unroll=2)
 
     def node_update(rows_state, own_part, summed, weight_sum, weight_out, gain):
         inner = own_part + dot(summed.astype(BF), weight_sum)
         return (rows_state.astype(F32) + normed(dot(silu(inner), weight_out), gain)).astype(BF)
 
-    summed = dot(sum_e[...], msgs[0:ENC, :])
-    state[...] = node_update(mlat[...], dot(mlat[...], encw[4]), summed, encw[5], encw[6], encg[1:2, :])
+    def mesh_update(old, count, sums, messages, weights, gain, turn):
+        def update(rows):
+            summed = dot(sums[0:rows, :], messages)
+            return node_update(
+                old[0:rows, :], node[0:rows, :], summed, weights[5], weights[6], gain
+            )
+
+        if turn < LAYERS:
+            loaded("mw0" if turn == 0 else "mw1")
+            coarse[turn, x, core, z, y] = dot(update(CO), mw[turn, 1]).astype(BF)
+            ag_start(turn)
+        state[...] = update(count)
+
+    mesh_update(mlat, M, sum_e, msgs[0:ENC, :], encw, encg[1:2, :], 0)
 
     loaded("mg", "medge")
     for layer in range(LAYERS):
         turn = layer + 1
-        loaded("mw0" if layer == 0 else "mw1")
         weights = [mw.at[layer, k] for k in range(7)]
         now = state[...]
         send = dot(now, weights[1][...]).astype(BF)
         mown[layer] = send
-        coarse[layer, x, core, z, y] = send[0:CO]
-        ag_start(layer)
         recv[...] = dot(now, weights[2][...]).astype(BF)
         node[0:M, :] = dot(now, weights[4][...])
 
@@ -367,15 +387,20 @@
             before[rows, :] = dot(left, right)
             return 0
 
-        lax.fori_loop(0, EDGES // BLOCK, first_part, 0, unroll=4)
         ag_second(layer)
         rim_start(mown.at[layer], mrim.at[layer], RIM_M, turn)
+        lax.fori_loop(0, EDGES // BLOCK, first_part, 0, unroll=4)
+        if layer == 0:
+            rim_sent(gown, grim, RIM_G, 0)
+        else:
+            ag_sent(layer - 1)
+            rim_sent(mown.at[layer - 1], mrim.at[layer - 1], RIM_M, layer)
         ag_third(layer)
         rim_wait(mown.at[layer], mrim.at[layer], RIM_M, turn)
         ag_last(layer)
 
         def second_part(n, _):
-            rows = pl.ds(pl.multiple_of(n * BLOCK, BLOCK), BLOCK)
+            rows = pl.ds(pl.multiple_of(n * WIDE, WIDE), WIDE)
             right = jnp.concatenate([mrim[layer], coarse[layer].reshape(8 * 16 * CO, L)], axis=0)
             hidden = silu(before[rows, :] + dot(hot_m[rows, 2 * M :], right))
             message = normed(dot(hidden, weights[3][...]), mg[layer, 0:1, :])
@@ -384,9 +409,8 @@
             msgs[rows, :] = message.astype(BF)
             return 0
 
-        lax.fori_loop(0, EDGES // BLOCK, second_part, 0, unroll=4)
-        summed = dot(sum_m[...], msgs[...])
-        state[...] = node_update(now, node[0:M, :], summed, weights[5][...], weights[6][...], mg[layer, 1:2, :])
+        lax.fori_loop(0, EDGES // WIDE, second_part, 0, unroll=4)
+        mesh_update(state, M, sum_m, msgs[...], mw.at[layer], mg[layer, 1:2, :], turn)
 
     mesh_out = pltpu.make_async_copy(state, mout_h, out_sem.at[0])
     mesh_out.start()
@@ -394,7 +418,6 @@
     mown[2] = dot(state[...], decw[1]).astype(BF)
     rim_start(mown.at[2], mrim.at[2], RIM_M, 3)
     node[...] = dot(glat[...], decw[4])
-    rim_sent(gown, grim, RIM_G, 0)
     gown[...] = dot(glat[...], decw[2]).astype(BF)
 
     edge = lax.broadcasted_iota(I32, (DEC_BLOCK, NODE_BLOCK), 0) - 3 * lax.broadcasted_iota(
@@ -414,7 +437,9 @@
         before[rows, :] = dot(left, right)
         return 0
 
-    lax.fori_loop(0, DEC // DEC_BLOCK, decode_first, 0, unroll=4)
+    lax.fori_loop(0, DEC // DEC_BLOCK, decode_first, 0, unroll=2)
+    ag_sent(LAYERS - 1)
+    rim_sent(mown.at[LAYERS - 1], mrim.at[LAYERS - 1], RIM_M, LAYERS)
     rim_wait(mown.at[2], mrim.at[2], RIM_M, 3)
 
     def decode_second(n, _):
@@ -428,13 +453,10 @@
         )
         return 0
 
-    lax.fori_loop(0, DEC // DEC_BLOCK, decode_second, 0, unroll=4)
+    lax.fori_loop(0, DEC // DEC_BLOCK, decode_second, 0, unroll=2)
     grid_out = pltpu.make_async_copy(mout, gout_h, out_sem.at[1])
     grid_out.start()
 
-    for layer in range(LAYERS):
-        ag_sent(layer)
-        rim_sent(mown.at[layer], mrim.at[layer], RIM_M, layer + 1)
     rim_sent(mown.at[2], mrim.at[2], RIM_M, 3)
     mesh_out.wait()
     grid_out.wait()

time: 81.5 us -> 76.9 us (0.944)
  Pallas kernels: 80.6 us -> 76.1 us
    pallas_call x1, Pallas kernels: 78.5 us -> 74.1 us  [per_device(): pl.pallas_call(kernel, out_shape=(jax.ShapeDtypeStruct((G, L), BF), jax.S...]
where the time goes in v2:
time: 76.9 us; the launch traced here: 76.8 us
  Pallas kernels  76.1 us (99%)
    pallas_call x1, Pallas kernels, per_device(): pl.pallas_call(kernel, out_shape=(jax.ShapeDtypeStruct((G, L), BF), jax.S...  74.1 us
    pallas_call x1, Pallas kernels, per_device(): pl.pallas_call(hand_on, out_shape=(jax.ShapeDtypeStruct((G, L), BF), jax....  2.02 us

profile of v2, /device:TPU:1, one launch (start us, length us, event | category | flops | bytes accessed | tf_op | source)
XLA Modules:
  0.0 76.8 jit_solution(4032623218035768048)
XLA Ops:
  0.6 74.1 %shard_map.194 = (bf16[512,512]{1,0:T(8,128)(2,1)}, bf16[256,512]{1,0:T(8,128)(2,1)}) custom-call(bf16[474,512]{1,0:T(8,128)(2,1)} %bitcast.19, bf16[256,512]{1,0:T(8,128)(2,1)} %bitcast.20, bf16[1024,512]{1,0:T(8,128)(2,1)} %bitcast.17, s32[1,1024]{1,0:T(1,128)} %bitcast.25, s32[1,1024]{1,0:T(1,128)} %bitcast.26, bf16[2048,512]{1,0:T(8,128)(2,1)} %bitcast.15, ...), custom_call_target="tpu_custom_call" | custom-call | flops 60000002048 | bytes 21000000 | tf_op jit(solution)/shard_map/pallas_call | solution.py:510
  74.7 2.0 %shard_map.195 = (bf16[512,512]{1,0:T(8,128)(2,1)}, bf16[256,512]{1,0:T(8,128)(2,1)}) custom-call(bf16[512,512]{1,0:T(8,128)(2,1)} %get-tuple-element.6.grid_in, bf16[256,512]{1,0:T(8,128)(2,1)} %get-tuple-element.7.mesh_in), custom_call_target="tpu_custom_call" | custom-call | tf_op jit(solution)/shard_map/pallas_call | solution.py:526

commit v3 on v2

--- a/solution.py
+++ b/solution.py
@@ -205,13 +205,11 @@
     def line_come(turn, dg, k):
         return ag_copy(turn, group(turn, back(g - dg), back(t - k)), 16 + dg * 4 + k, partner)
 
-    def core_send(turn, dg, k):
-        return ag_copy(turn, group(turn, back(g - dg), back(t - k)), 32 + dg * 4 + k, partner)
-
-    def core_come(turn, dg, k):
-        gv, tv = back(t - dg), back(g - k)
-        piece = coarse.at[turn, pick(gv, tv), 1 - core, pick(tv, gv)]
-        return ag_copy(turn, piece, 32 + dg * 4 + k, partner)
+    def core_send(turn, v):
+        return ag_copy(turn, coarse.at[turn, v, core], 32 + v, partner)
+
+    def core_come(turn, v):
+        return ag_copy(turn, coarse.at[turn, v, 1 - core], 32 + v, partner)
 
     def ag_start(turn):
         for dg, dy in plane:
@@ -224,27 +222,25 @@
                     plane_come(turn, dg, dy).wait_recv()
             for k in (2, 1, 3):
                 line_send(turn, dg, k).start()
-            core_send(turn, dg, 0).start()
 
     def ag_third(turn):
         for dg in (0, 1, 3, 2):
             for k in (1, 3, 2):
                 line_come(turn, dg, k).wait_recv()
-                core_send(turn, dg, k).start()
+        for v in range(4):
+            core_send(turn, v).start()
 
     def ag_last(turn):
-        for dg in (0, 1, 3, 2):
-            for k in (0, 1, 3, 2):
-                core_come(turn, dg, k).wait_recv()
+        for v in range(4):
+            core_come(turn, v).wait_recv()
 
     def ag_sent(turn):
         for dg, dy in plane:
             plane_send(turn, dg, dy).wait_send()
         for dg in range(4):
-            for k in range(4):
-                if k:
-                    line_send(turn, dg, k).wait_send()
-                core_send(turn, dg, k).wait_send()
+            for k in range(1, 4):
+                line_send(turn, dg, k).wait_send()
+            core_send(turn, dg).wait_send()
 
     loaded("feat", "ew1")
     hidden = silu(
@@ -397,12 +393,29 @@
             rim_sent(mown.at[layer - 1], mrim.at[layer - 1], RIM_M, layer)
         ag_third(layer)
         rim_wait(mown.at[layer], mrim.at[layer], RIM_M, turn)
+
+        def half(rows, on):
+            columns = [
+                hot_m[rows, pl.ds(pl.multiple_of((3 + 2 * v + on) * M, M), M)] for v in range(4)
+            ]
+            table = [coarse[layer, v, on].reshape(16 * CO, L) for v in range(4)]
+            return columns, table
+
+        def own_half(n, _):
+            rows = pl.ds(pl.multiple_of(n * WIDE, WIDE), WIDE)
+            columns, table = half(rows, core)
+            left = jnp.concatenate([hot_m[rows, 2 * M : 3 * M]] + columns, axis=1)
+            before[rows, :] += dot(left, jnp.concatenate([mrim[layer]] + table, axis=0))
+            return 0
+
+        lax.fori_loop(0, EDGES // WIDE, own_half, 0, unroll=2)
         ag_last(layer)
 
         def second_part(n, _):
             rows = pl.ds(pl.multiple_of(n * WIDE, WIDE), WIDE)
-            right = jnp.concatenate([mrim[layer], coarse[layer].reshape(8 * 16 * CO, L)], axis=0)
-            hidden = silu(before[rows, :] + dot(hot_m[rows, 2 * M :], right))
+            columns, table = half(rows, 1 - core)
+            left, right = jnp.concatenate(columns, axis=1), jnp.concatenate(table, axis=0)
+            hidden = silu(before[rows, :] + dot(left, right))
             message = normed(dot(hidden, weights[3][...]), mg[layer, 0:1, :])
             if layer + 1 < LAYERS:
                 medge[rows, :] = (medge[rows, :].astype(F32) + message).astype(BF)
@@ -504,8 +517,8 @@
         pltpu.SemaphoreType.DMA((2,)),
         pltpu.SemaphoreType.DMA((4, 8)),
         pltpu.SemaphoreType.DMA((4, 8)),
-        pltpu.SemaphoreType.DMA((LAYERS, 48)),
-        pltpu.SemaphoreType.DMA((LAYERS, 48)),
+        pltpu.SemaphoreType.DMA((LAYERS, 36)),
+        pltpu.SemaphoreType.DMA((LAYERS, 36)),
     ]
     grid_out, mesh_out = pl.pallas_call(
         kernel,

time: 76.9 us -> 76.7 us (level)
  no operation moved by 1% of the time
where the time goes in v3:
time: 76.7 us; the launch traced here: 76.6 us
  Pallas kernels  75.9 us (99%)
    pallas_call x1, Pallas kernels, per_device(): pl.pallas_call(kernel, out_shape=(jax.ShapeDtypeStruct((G, L), BF), jax.S...  73.9 us
    pallas_call x1, Pallas kernels, per_device(): pl.pallas_call(hand_on, out_shape=(jax.ShapeDtypeStruct((G, L), BF), jax....  2.02 us

profile of v3, /device:TPU:1, one launch (start us, length us, event | category | flops | bytes accessed | tf_op | source)
XLA Modules:
  0.0 76.6 jit_solution(17119835321234188959)
XLA Ops:
  0.6 73.9 %shard_map.194 = (bf16[512,512]{1,0:T(8,128)(2,1)}, bf16[256,512]{1,0:T(8,128)(2,1)}) custom-call(bf16[474,512]{1,0:T(8,128)(2,1)} %bitcast.19, bf16[256,512]{1,0:T(8,128)(2,1)} %bitcast.20, bf16[1024,512]{1,0:T(8,128)(2,1)} %bitcast.17, s32[1,1024]{1,0:T(1,128)} %bitcast.25, s32[1,1024]{1,0:T(1,128)} %bitcast.26, bf16[2048,512]{1,0:T(8,128)(2,1)} %bitcast.15, ...), custom_call_target="tpu_custom_call" | custom-call | flops 60000002048 | bytes 21000000 | tf_op jit(solution)/shard_map/pallas_call | solution.py:523
  74.6 2.0 %shard_map.195 = (bf16[512,512]{1,0:T(8,128)(2,1)}, bf16[256,512]{1,0:T(8,128)(2,1)}) custom-call(bf16[512,512]{1,0:T(8,128)(2,1)} %get-tuple-element.6.grid_in, bf16[256,512]{1,0:T(8,128)(2,1)} %get-tuple-element.7.mesh_in), custom_call_target="tpu_custom_call" | custom-call | tf_op jit(solution)/shard_map/pallas_call | solution.py:539
